TPU v7x, 1024 devices: a whole 4x4x32 slice. The times are simulated.
1024 devices in a mesh: wide: 64 (over z, core), narrow: 16 (over y, x).
Axes of the slice: x: 4, y: 4, z: 32, core: 2. Of those that a mesh axis runs over, the one named last changes fastest.
Arguments:
- audio: bfloat16 [131072, 1024], P(('wide', 'narrow')), may hold values from -0.25 to 0.25
- text: bfloat16 [131072, 1024], P(('wide', 'narrow')), may hold values from -0.25 to 0.25
- labels: int32 [131072], P(('wide', 'narrow')), may hold values from 0 to 32767
- route: int32 [131072, 1], P(('wide', 'narrow')), may hold values from 0 to 63; in each aligned block of 128 rows (0 to 127, 128 to 255, ...) at most 4 rows name the same one
- scale: float32 [1], replicated, may hold values from 8 to 16
- bias: float32 [1], replicated, may hold values from -2 to 0
Outputs:
- row_loss: float32 [131072], P(('wide', 'narrow'))
- audio_grad: float32 [131072, 1024], P(('wide', 'narrow'))
- text_grad: float32 [131072, 1024], P(('wide', 'narrow'))
Inputs may be any that keep to these rules, and one draw needn't show every extreme that they name: route[j, 0] is a wide index; the holder has the narrow index of j's device. No device names one wide index with more than 4 of its rows, and some device names some wide index with exactly 4.
All inputs are finite; a program needn't handle non-finite values.
Results may differ from a plain program's by a relative error of at most 0.0045.
Values may be sent and summed in bfloat16 or wider, within the bound.
A program may use at most 64 MiB of HBM per device.

v0:
```python
import jax
import jax.numpy as jnp
from jax import lax
from jax.sharding import PartitionSpec as P

EPSILON = 1e-06


def unit_rows(raw):
    values = raw.astype(jnp.float32)
    length = jnp.sqrt(jnp.sum(values * values, axis=-1, keepdims=True) + EPSILON)
    return (values / length, length)


def back_through_norm(unit, length, grad):
    return (grad - unit * jnp.sum(unit * grad, axis=-1, keepdims=True)) / length


def tile_terms(audio_hat, audio_labels, text_block, text_labels, scale_value, bias_value):
    logits = (
        scale_value * jnp.dot(audio_hat, text_block.T, preferred_element_type=jnp.float32)
        + bias_value
    )
    matched = audio_labels[:, None] == text_labels[None, :]
    present = (text_labels >= 0)[None, :]
    signed = jnp.where(matched, 1.0, -1.0).astype(jnp.float32)
    losses = jnp.where(present, jax.nn.softplus(-signed * logits), 0.0)
    slope = jnp.where(present, jax.nn.sigmoid(logits) - matched.astype(jnp.float32), 0.0)
    weights = (scale_value * slope).astype(jnp.bfloat16)
    grad_audio = jnp.dot(weights, text_block, preferred_element_type=jnp.float32)
    grad_text = jnp.dot(weights.T, audio_hat, preferred_element_type=jnp.float32)
    return (jnp.sum(losses, axis=1), grad_audio, grad_text)


def body(audio, text, labels, route, scale, bias):
    row_count = audio.shape[0]
    width = audio.shape[1]
    wide_size = lax.axis_size("wide")
    narrow_size = lax.axis_size("narrow")
    capacity = max(2, 2 * row_count // wide_size)
    slots = wide_size * capacity
    group = row_count * narrow_size
    audio_unit, audio_len = unit_rows(audio)
    text_unit, text_len = unit_rows(text)
    audio_hat = audio_unit.astype(jnp.bfloat16)
    text_hat = text_unit.astype(jnp.bfloat16)
    scale_value = scale[0]
    bias_value = bias[0]
    target = route[:, 0]
    order = jnp.arange(row_count, dtype=jnp.int32)
    earlier = (target[:, None] == target[None, :]) & (order[:, None] > order[None, :])
    slot_rank = jnp.sum(earlier.astype(jnp.int32), axis=1)
    position = target * capacity + slot_rank
    send_text = jnp.zeros((slots, width), jnp.bfloat16).at[position].set(text_hat)
    send_text = send_text.reshape(wide_size, capacity, width)
    send_labels = jnp.full((slots,), -1, jnp.int32).at[position].set(labels)
    send_labels = send_labels.reshape(wide_size, capacity)
    routed_text, routed_labels = (
        lax.all_to_all(send_text, "wide", split_axis=0, concat_axis=0, tiled=True),
        lax.all_to_all(send_labels, "wide", split_axis=0, concat_axis=0, tiled=True),
    )
    group_text, group_labels = (
        lax.all_gather(text_hat, "narrow", axis=0, tiled=True),
        lax.all_gather(labels, "narrow", axis=0, tiled=True),
    )
    own_loss, own_audio, group_text_grad = tile_terms(
        audio_hat, labels, group_text, group_labels, scale_value, bias_value
    )
    own_text = lax.psum_scatter(group_text_grad, "narrow", scatter_dimension=0, tiled=True)
    routed_text = routed_text.reshape(slots, width)
    routed_labels = routed_labels.reshape(slots)
    far_loss, far_audio, far_text = tile_terms(
        audio_hat, labels, routed_text, routed_labels, scale_value, bias_value
    )
    reply = far_text.astype(jnp.bfloat16).reshape(wide_size, capacity, width)
    returned = lax.all_to_all(reply, "wide", split_axis=0, concat_axis=0, tiled=True)
    remote = returned.reshape(slots, width)[position].astype(jnp.float32)
    row_loss = (own_loss + far_loss) / group
    audio_grad = back_through_norm(audio_unit, audio_len, own_audio + far_audio)
    text_grad = back_through_norm(text_unit, text_len, own_text + remote)
    return (row_loss, audio_grad, text_grad)


def solution(mesh):
    return jax.shard_map(
        body,
        mesh=mesh,
        in_specs=(
            P(("wide", "narrow"), None),
            P(("wide", "narrow"), None),
            P(("wide", "narrow")),
            P(("wide", "narrow"), None),
            P(),
            P(),
        ),
        out_specs=(P(("wide", "narrow")), P(("wide", "narrow"), None), P(("wide", "narrow"), None)),
        check_vma=False,
    )
```

profile of v0, /device:TPU:1, one launch (start us, length us, event | category | flops | bytes accessed | tf_op | source)
XLA Modules:
  0.0 319.1 jit_solution(15671857065111516361)
XLA Ops:
  7.2 1.1 fusion.11
  8.3 1.8 fusion.27
  11.5 17.2 %all-gather = s32[16,1,128]{2,1,0:T(1,128)S(1)} all-gather(s32[1,1,128]{2,1,0:T(1,128)} %bitcast.28), channel_id=1, replica_groups=mesh['wide'=64,'narrow'=16] {'narrow'}, dimensions={0}, use_global_device_ids=true | all-gather | bytes 8704 | tf_op jit(solution)/shard_map/all_gather | solution.py:64
  28.7 1.1 fusion.10
  29.8 78.7 %all-gather.3.cloned.1.call-done = bf16[2048,1024]{1,0:T(8,128)(2,1)} async-done(((bf16[128,1024]{1,0:T(8,128)(2,1)}), bf16[2048,1024]{1,0:T(8,128)(2,1)}) %all-gather.3.cloned.1.call-update) | async-done | bytes 4194320 | tf_op jit(solution)/shard_map/all_gather | solution.py:63
  108.5 4.5 %fusion.9 = (f32[128]{0:T(128)S(1)}, f32[128,2048]{1,0:T(8,128)S(1)}) fusion(s32[2048]{0:T(1024)S(1)} %bitcast.25, s32[128]{0:T(128)} %param.8, pred[2048]{0:T(1024)(128)(4,1)S(1)} %broadcast_compare_fusion, f32[]{:T(128)} %bitcast.22, bf16[2048,1024]{1,0:T(8,128)(2,1)} %all-gather.3.cloned.1.call-done, f32[128]{0:T(128)S(1)} %add_sqrt_fusion.1, ...), kind=kOutput, calls=%fused_computation.19 | convolution fusion | flops 540934016 | bytes 5516808 | tf_op jit(solution)/shard_map/dot_general | solution.py:21
  113.0 4.7 %fusion.32 = f32[2048,1024]{1,0:T(8,128)} fusion(f32[128]{0:T(128)S(1)} %add_sqrt_fusion.1, bf16[128,1024]{1,0:T(8,128)(2,1)S(1)} %copy-done.1, f32[128,2048]{1,0:T(8,128)S(1)} %get-tuple-element.4, f32[]{:T(128)} %bitcast.21, s32[2048]{0:T(1024)S(1)} %bitcast.26, s32[128]{0:T(128)S(1)} %copy-done.2, pred[2048]{0:T(1024)(128)(4,1)S(1)} %broadcast_compare_fusion), kind=kOutput, calls=%fused_computation.61 | convolution fusion | flops 539623424 | bytes 9710596 | tf_op jit(solution)/shard_map/dot_general | solution.py:31
  117.8 0.6 copy-done.3
  118.4 0.2 convert_reduce_fusion
  118.6 1.0 scatter_custom_fusion
  119.6 0.7 all_to_all.12
  120.3 23.8 %all-to-all-start = ((s32[64,1,4]{2,1,0:T(1,128)}), s32[64,1,4]{2,1,0:T(1,128)S(1)}, u32[]{:S(2)}, u32[]{:S(2)}) async-start(s32[64,1,4]{2,1,0:T(1,128)} %bitcast.7), calls=%async_computation | async-start | bytes 65536 | tf_op jit(solution)/shard_map/all_to_all | solution.py:60
  144.1 1.4 scatter_custom_fusion.1
  145.5 1.0 reshape.53
  146.5 20.0 %all-to-all-done = s32[64,1,4]{2,1,0:T(1,128)S(1)} async-done(((s32[64,1,4]{2,1,0:T(1,128)}), s32[64,1,4]{2,1,0:T(1,128)S(1)}, u32[]{:S(2)}, u32[]{:S(2)}) %all-to-all-start) | async-done | bytes 1056 | tf_op jit(solution)/shard_map/all_to_all | solution.py:60
  166.4 5.7 %all-to-all-start.1 = ((bf16[64,4,1024]{2,1,0:T(4,128)(2,1)}), bf16[64,4,1024]{2,1,0:T(4,128)(2,1)S(1)}, u32[]{:S(2)}, u32[]{:S(2)}) async-start(bf16[64,4,1024]{2,1,0:T(4,128)(2,1)} %reshape.53), calls=%async_computation.1 | async-start | bytes 1048576 | tf_op jit(solution)/shard_map/all_to_all | solution.py:59
  172.1 0.5 broadcast.48
  172.6 0.7 reduce.3
  173.5 63.0 %all-to-all-done.1 = bf16[64,4,1024]{2,1,0:T(4,128)(2,1)S(1)} async-done(((bf16[64,4,1024]{2,1,0:T(4,128)(2,1)}), bf16[64,4,1024]{2,1,0:T(4,128)(2,1)S(1)}, u32[]{:S(2)}, u32[]{:S(2)}) %all-to-all-start.1) | async-done | bytes 524320 | tf_op jit(solution)/shard_map/all_to_all | solution.py:59
  236.5 0.1 reshape.54
  236.6 0.5 fusion.21
  237.1 0.4 convolution_convert_fusion
  237.5 1.0 reshape.55
  238.5 5.0 %all-to-all-start.2 = ((bf16[64,4,1024]{2,1,0:T(4,128)(2,1)}), bf16[64,4,1024]{2,1,0:T(4,128)(2,1)S(1)}, u32[]{:S(2)}, u32[]{:S(2)}) async-start(bf16[64,4,1024]{2,1,0:T(4,128)(2,1)} %reshape.55), calls=%async_computation.3 | async-start | bytes 1048576 | tf_op jit(solution)/shard_map/all_to_all | solution.py:76
  243.5 0.3 fusion.29
  243.8 0.5 add_multiply_fusion
  244.3 3.2 %multiply_reduce_fusion.1 = (f32[128]{0:T(128)S(1)}, f32[128,1024]{1,0:T(8,128)S(1)}) fusion(f32[128]{0:T(128)S(1)} %add_sqrt_fusion.1, bf16[128,1024]{1,0:T(8,128)(2,1)S(1)} %copy-done.1, f32[128,1024]{1,0:T(8,128)S(1)} %fusion.29, bf16[2048,1024]{1,0:T(8,128)(2,1)} %all-gather.3.cloned.1.call-done, f32[128,2048]{1,0:T(8,128)S(1)} %get-tuple-element.4, ...), kind=kOutput, calls=%fused_computation.30 | convolution fusion | flops 539885440 | bytes 6565380 | tf_op jit(solution)/shard_map/dot_general | solution.py:30
  247.6 1.0 subtract_divide_fusion.1
  248.6 59.4 %all-to-all-done.2 = bf16[64,4,1024]{2,1,0:T(4,128)(2,1)S(1)} async-done(((bf16[64,4,1024]{2,1,0:T(4,128)(2,1)}), bf16[64,4,1024]{2,1,0:T(4,128)(2,1)S(1)}, u32[]{:S(2)}, u32[]{:S(2)}) %all-to-all-start.2) | async-done | bytes 524320 | tf_op jit(solution)/shard_map/all_to_all | solution.py:76
  308.1 0.9 gather_fusion
  308.9 1.3 multiply_reduce_fusion
  310.2 2.0 subtract_divide_fusion
  (20 shorter events, 0.4 us)
Async XLA Ops:
  7.2 101.4 %all-gather.3.cloned.1.call-start = ((), (), s32[]{:S(2)}) async-start(), calls=%async_computation.4 | async-start | bytes 4456448 | tf_op jit(solution)/shard_map/all_gather | solution.py:63
  10.1 298.8 %reduce-scatter.2.cloned.1.call-start = ((), (), s32[]{:S(2)}) async-start(), calls=%async_computation.5 | async-start | bytes 8912896 | tf_op jit(solution)/shard_map/reduce_scatter | solution.py:69
  108.5 4.5 %copy-start.1 = (bf16[128,1024]{1,0:T(8,128)(2,1)S(1)}, bf16[128,1024]{1,0:T(8,128)(2,1)}, u32[]{:S(2)}) copy-start(bf16[128,1024]{1,0:T(8,128)(2,1)} %param.6) | copy-start | bytes 786436
  108.5 4.5 %copy-start.2 = (s32[128]{0:T(128)S(1)}, s32[128]{0:T(128)}, u32[]{:S(2)}) copy-start(s32[128]{0:T(128)} %param.8) | copy-start | bytes 1540
  117.8 0.7 copy-start.3
  117.8 26.3 %copy-start = (bf16[128,1024]{1,0:T(8,128)(2,1)S(1)}, bf16[128,1024]{1,0:T(8,128)(2,1)}, u32[]{:S(2)}) copy-start(bf16[128,1024]{1,0:T(8,128)(2,1)} %param.7) | copy-start | bytes 786436
  120.3 46.1 %all-to-all-start = ((s32[64,1,4]{2,1,0:T(1,128)}), s32[64,1,4]{2,1,0:T(1,128)S(1)}, u32[]{:S(2)}, u32[]{:S(2)}) async-start(s32[64,1,4]{2,1,0:T(1,128)} %bitcast.7), calls=%async_computation | async-start | bytes 65536 | tf_op jit(solution)/shard_map/all_to_all | solution.py:60
  166.4 70.1 %all-to-all-start.1 = ((bf16[64,4,1024]{2,1,0:T(4,128)(2,1)}), bf16[64,4,1024]{2,1,0:T(4,128)(2,1)S(1)}, u32[]{:S(2)}, u32[]{:S(2)}) async-start(bf16[64,4,1024]{2,1,0:T(4,128)(2,1)} %reshape.53), calls=%async_computation.1 | async-start | bytes 1048576 | tf_op jit(solution)/shard_map/all_to_all | solution.py:59
  238.5 69.4 %all-to-all-start.2 = ((bf16[64,4,1024]{2,1,0:T(4,128)(2,1)}), bf16[64,4,1024]{2,1,0:T(4,128)(2,1)S(1)}, u32[]{:S(2)}, u32[]{:S(2)}) async-start(bf16[64,4,1024]{2,1,0:T(4,128)(2,1)} %reshape.55), calls=%async_computation.3 | async-start | bytes 1048576 | tf_op jit(solution)/shard_map/all_to_all | solution.py:76
Sparse Core Ops, SparseCore 0:
  12.7 95.7 all-gather.2
  117.9 119.7 reduce-scatter.1
where the time goes:
time: 320 us; the launch traced here: 319 us
  waiting for transfers between devices  221 us (69%)
  starting transfers between devices  34.5 us (11%)
  blocking collectives  17.2 us (5%)
  between operations  15.5 us (5%)
  matrix products  13.6 us (4%)
  other arithmetic  11.1 us (3%)
  local copies, waits for them, and re-layouts  6.03 us (2%)
    all_gather x1, waiting for transfers between devices, body(): lax.all_gather(text_hat, 'narrow', axis=0, tiled=True)  78.7 us
    all_to_all x1, waiting for transfers between devices, body(): lax.all_to_all(send_text, 'wide', split_axis=0, concat_axis=0, tiled=True)  63 us
    all_to_all x1, waiting for transfers between devices, body(): lax.all_to_all(reply, 'wide', split_axis=0, concat_axis=0, tiled=True)  59.4 us
    all_to_all x1, starting transfers between devices, body(): lax.all_to_all(send_labels, 'wide', split_axis=0, concat_axis=0, tiled=True)  23.8 us
    all_to_all x1, waiting for transfers between devices, body(): lax.all_to_all(send_labels, 'wide', split_axis=0, concat_axis=0, tiled=True)  20 us
    all_gather x1, blocking collectives, body(): lax.all_gather(labels, 'narrow', axis=0, tiled=True)  17.2 us
  transfers between devices with their start and end apart: 5, of which 4 were waited for; matrix products, arithmetic and copies ran while one was open for 4% of the time, Pallas kernels for 0%

commit v1 on v0

v1 whole, which is shorter than its diff:
```python
import functools
import math

import jax
import jax.numpy as jnp
from jax import lax
from jax.experimental import pallas as pl
from jax.experimental.pallas import tpu as pltpu
from jax.sharding import PartitionSpec as P

EPSILON = 1e-06
MESH = pl.DeviceIdType.MESH
LANES = 128
CAPACITY = 4
F32 = jnp.float32
BF16 = jnp.bfloat16


def unit_rows(raw):
    values = raw.astype(F32)
    length = jnp.sqrt(jnp.sum(values * values, axis=-1, keepdims=True) + EPSILON)
    return (values / length, length)


def back_through_norm(unit, length, grad):
    return (grad - unit * jnp.sum(unit * grad, axis=-1, keepdims=True)) / length


def dot_nt(a, b):
    return lax.dot_general(a, b, (((1,), (1,)), ((), ())), preferred_element_type=F32)


def dot_nn(a, b):
    return lax.dot_general(a, b, (((1,), (0,)), ((), ())), preferred_element_type=F32)


def dot_tn(a, b):
    return lax.dot_general(a, b, (((0,), (0,)), ((), ())), preferred_element_type=F32)


def iota(shape, axis):
    return lax.broadcasted_iota(jnp.int32, shape, axis)


def to_column(row):
    size = row.shape[1]
    eye = iota((size, size), 0) == iota((size, size), 1)
    return jnp.sum(jnp.where(eye, row, 0.0), axis=1, keepdims=True)


def to_row(column):
    size = column.shape[0]
    eye = iota((size, size), 0) == iota((size, size), 1)
    return jnp.sum(jnp.where(eye, column, 0.0), axis=0, keepdims=True)


def pair_terms(products, audio_labels, text_labels, scale, bias):
    logits = scale * products + bias
    matched = audio_labels == text_labels
    small = jnp.exp(-jnp.abs(logits))
    losses = jnp.maximum(jnp.where(matched, -logits, logits), 0.0) + jnp.log1p(small)
    sigmoid = jnp.where(logits >= 0.0, 1.0, small) / (1.0 + small)
    slope = sigmoid - jnp.where(matched, 1.0, 0.0)
    return (losses, slope)


def write_blocks(slab, out_ref, chunks):
    for half in range(chunks // 4):
        even, odd = [], []
        for g in (2 * half, 2 * half + 1):
            first, second = slab(2 * g), slab(2 * g + 1)
            first = first.reshape(-1, 8, LANES)
            second = second.reshape(-1, 8, LANES)
            low = iota(first.shape, 1) < CAPACITY
            even.append(jnp.where(low, first, pltpu.roll(second, CAPACITY, 1)))
            odd.append(jnp.where(low, pltpu.roll(first, CAPACITY, 1), second))
        rows = pl.ds(16 * half, 16)
        out_ref[:, 0, rows, :] = jnp.concatenate(even, axis=1).astype(BF16)
        out_ref[:, 1, rows, :] = jnp.concatenate(odd, axis=1).astype(BF16)


def read_blocks(in_ref, out_ref, chunks):
    for half in range(chunks // 4):
        rows = pl.ds(16 * half, 16)
        even = in_ref[:, 0, rows, :].astype(F32)
        odd = in_ref[:, 1, rows, :].astype(F32)
        for step in range(2):
            g = 2 * half + step
            e = even[:, 8 * step : 8 * step + 8, :]
            o = odd[:, 8 * step : 8 * step + 8, :]
            low = iota(e.shape, 1) < CAPACITY
            first = jnp.where(low, e, pltpu.roll(o, CAPACITY, 1))
            second = jnp.where(low, pltpu.roll(e, CAPACITY, 1), o)
            out_ref[:, pl.ds(2 * g * LANES, LANES)] = first.reshape(-1, LANES).astype(BF16)
            out_ref[:, pl.ds((2 * g + 1) * LANES, LANES)] = second.reshape(-1, LANES).astype(BF16)


def kernel(
    wide_size, side,
    scale_ref, bias_ref, audio_ref, text_ref, labels_ref, route_ref,
    loss_ref, audio_grad_ref, text_grad_ref,
    out_rows, in_rows, out_reply, in_reply, out_labels, in_labels, slots,
    audio_all, text_all, audio_labels, text_labels,
    weights, audio_sum, text_sum, loss_sum,
    audio_out, audio_in, text_out, text_in, loss_out, loss_in,
    rows_send, rows_recv, labels_send, labels_recv, reply_send, reply_recv,
    near_send, near_recv, local_sem,
):
    row_count, width = audio_ref.shape
    chunks = width // LANES
    group = row_count * side * side
    slot_count = wide_size * CAPACITY
    w = lax.axis_index("wide")
    n = lax.axis_index("narrow")
    y, x = n // side, n % side
    scale, bias = scale_ref[0], bias_ref[0]

    def far(k):
        return lax.rem(w + k, wide_size)

    def along_x(d):
        return lax.rem(x + d, side)

    def along_y(d):
        return lax.rem(y + d, side)

    barrier = pltpu.get_barrier_semaphore()

    def greet(k, carry):
        pl.semaphore_signal(barrier, inc=1, device_id=(far(k), n), device_id_type=MESH)
        return carry

    lax.fori_loop(1, wide_size, greet, 0)
    for d in range(1, side):
        pl.semaphore_signal(barrier, inc=1, device_id=(w, y * side + along_x(d)), device_id_type=MESH)
        pl.semaphore_signal(barrier, inc=1, device_id=(w, along_y(d) * side + x), device_id_type=MESH)

    text_hat = unit_rows(text_ref[...])[0].astype(BF16)
    text_all[y] = text_hat
    label_row = labels_ref[...].astype(F32)
    text_labels[y] = label_row
    audio_labels[x] = label_row
    target = route_ref[...].astype(F32)
    target_row = to_row(target)
    square = (row_count, row_count)
    same = target == target_row
    before = iota(square, 0) < iota(square, 1)
    after = iota(square, 0) > iota(square, 1)
    rank_row = jnp.sum(jnp.where(same & before, 1.0, 0.0), axis=0, keepdims=True)
    rank = jnp.sum(jnp.where(same & after, 1.0, 0.0), axis=1, keepdims=True)
    place_row = (target_row * CAPACITY + rank_row).astype(jnp.int32)
    place = (target * CAPACITY + rank).astype(jnp.int32)
    pick = jnp.where(iota((slot_count, row_count), 0) == place_row, 1.0, 0.0).astype(BF16)
    write_blocks(lambda c: dot_nn(pick, text_hat[:, c * LANES : (c + 1) * LANES]), out_rows, chunks)
    holder = iota((wide_size, row_count), 0) * CAPACITY
    lane = iota((wide_size, LANES), 1)
    packed = jnp.full((wide_size, LANES), -1.0, F32)
    for k in range(CAPACITY):
        found = jnp.where(holder + k == place_row, label_row + 1.0, 0.0)
        packed = jnp.where(lane == k, jnp.sum(found, axis=1, keepdims=True) - 1.0, packed)
    out_labels[...] = packed.reshape(wide_size, 1, LANES)

    pl.semaphore_wait(barrier, wide_size - 1 + 2 * (side - 1))

    def block_copy(src, dst, send, recv, k):
        peer = far(k)
        return pltpu.make_async_remote_copy(
            src_ref=src.at[peer // 2, peer % 2],
            dst_ref=dst.at[w // 2, w % 2],
            send_sem=send.at[k],
            recv_sem=recv.at[k],
            device_id=(peer, n),
            device_id_type=MESH,
        )

    def label_copy(k):
        peer = far(k)
        return pltpu.make_async_remote_copy(
            src_ref=out_labels.at[peer],
            dst_ref=in_labels.at[w],
            send_sem=labels_send.at[k],
            recv_sem=labels_recv.at[k],
            device_id=(peer, n),
            device_id_type=MESH,
        )

    def each(start, make, act):
        def step(k, carry):
            act(make(k))
            return carry

        lax.fori_loop(start, wide_size, step, 0)

    def rows_copy(k):
        return block_copy(out_rows, in_rows, rows_send, rows_recv, k)

    def reply_copy(k):
        return block_copy(out_reply, in_reply, reply_send, reply_recv, k)

    def start(copy):
        copy.start()

    def arrived(copy):
        copy.wait_recv()

    def left(copy):
        copy.wait_send()

    each(1, rows_copy, start)
    each(1, label_copy, start)
    own_rows = pltpu.make_async_copy(out_rows.at[w // 2, w % 2], in_rows.at[w // 2, w % 2], local_sem.at[0])
    own_rows.start()
    own_labels = pltpu.make_async_copy(out_labels.at[w], in_labels.at[w], local_sem.at[1])
    own_labels.start()

    def near_copy(kind, src, dst, d, on_x):
        peer = y * side + along_x(d) if on_x else along_y(d) * side + x
        return pltpu.make_async_remote_copy(
            src_ref=src,
            dst_ref=dst,
            send_sem=near_send.at[kind, d],
            recv_sem=near_recv.at[kind, d],
            device_id=(w, peer),
            device_id_type=MESH,
        )

    near = []
    for d in range(1, side):
        near.append(near_copy(0, text_all.at[y], text_all.at[y], d, False))
        near.append(near_copy(1, text_labels.at[y], text_labels.at[y], d, False))
        near.append(near_copy(2, audio_labels.at[x], audio_labels.at[x], d, True))
    for copy in near:
        copy.start()
    audio_hat = unit_rows(audio_ref[...])[0].astype(BF16)
    audio_all[x] = audio_hat
    shared = [near_copy(3, audio_all.at[x], audio_all.at[x], d, True) for d in range(1, side)]
    for copy in shared:
        copy.start()
    near += shared
    for copy in near:
        copy.wait_recv()

    block_rows = side * row_count
    text_block = text_all[...].reshape(block_rows, width)
    column_labels = jnp.concatenate([text_labels[t] for t in range(side)], axis=1)
    sent = []
    for d in range(side):
        owner = along_x(d)
        rows = audio_all[owner]
        losses, slope = pair_terms(
            dot_nt(rows, text_block), to_column(audio_labels[owner]), column_labels, scale, bias
        )
        block = (scale * slope).astype(BF16)
        for t in range(side):
            weights[t, owner] = block[:, t * row_count : (t + 1) * row_count]
        grad = dot_nn(block, text_block)
        loss = to_row(jnp.sum(losses, axis=1, keepdims=True))
        if d == 0:
            audio_sum[...] = grad
            loss_sum[...] = loss
        else:
            audio_out[d - 1] = grad.astype(BF16)
            loss_out[d - 1] = loss
            sent.append(near_copy(4, audio_out.at[d - 1], audio_in.at[d - 1], d, True))
            sent.append(near_copy(5, loss_out.at[d - 1], loss_in.at[d - 1], d, True))
            sent[-2].start()
            sent[-1].start()
    audio_block = audio_all[...].reshape(block_rows, width)
    for d in range(side):
        grad = dot_tn(weights[along_y(d)].reshape(block_rows, row_count), audio_block)
        if d == 0:
            text_sum[...] = grad
        else:
            text_out[d - 1] = grad.astype(BF16)
            sent.append(near_copy(6, text_out.at[d - 1], text_in.at[d - 1], d, False))
            sent[-1].start()

    own_labels.wait()
    own_rows.wait()
    each(1, label_copy, arrived)
    each(1, rows_copy, arrived)
    read_blocks(in_rows, slots, chunks)
    received = in_labels[...].reshape(wide_size, LANES)
    holder_slot = iota((wide_size, slot_count), 0) * CAPACITY
    slot_lane = iota((wide_size, slot_count), 1)
    slot_labels = jnp.zeros((1, slot_count), F32)
    for k in range(CAPACITY):
        found = jnp.where(slot_lane == holder_slot + k, received[:, k : k + 1], 0.0)
        slot_labels += jnp.sum(found, axis=0, keepdims=True)
    own_audio = audio_all[x]
    held = slots[...]
    losses, slope = pair_terms(
        dot_nt(own_audio, held), to_column(audio_labels[x]), slot_labels, scale, bias
    )
    present = slot_labels >= 0.0
    routed = (scale * jnp.where(present, slope, 0.0)).astype(BF16)
    write_blocks(
        lambda c: dot_tn(routed, audio_all[x, :, pl.ds(c * LANES, LANES)]), out_reply, chunks
    )
    each(1, reply_copy, start)
    own_reply = pltpu.make_async_copy(out_reply.at[w // 2, w % 2], in_reply.at[w // 2, w % 2], local_sem.at[0])
    own_reply.start()

    loss_sum[...] += to_row(jnp.sum(jnp.where(present, losses, 0.0), axis=1, keepdims=True))
    audio_sum[...] += dot_nn(routed, held)
    for copy in sent:
        copy.wait_recv()
    total = audio_sum[...]
    loss = loss_sum[...]
    for d in range(side - 1):
        total += audio_in[d].astype(F32)
        loss += loss_in[d]
    loss_ref[...] = loss / group
    audio_unit, audio_len = unit_rows(audio_ref[...])
    audio_grad_ref[...] = back_through_norm(audio_unit, audio_len, total)
    for d in range(side - 1):
        text_sum[...] += text_in[d].astype(F32)
    for copy in near + sent:
        copy.wait_send()
    each(1, rows_copy, left)
    each(1, label_copy, left)

    own_reply.wait()
    each(1, reply_copy, arrived)
    read_blocks(in_reply, slots, chunks)
    pick_back = jnp.where(iota((row_count, slot_count), 1) == place, 1.0, 0.0).astype(BF16)
    total = text_sum[...] + dot_nn(pick_back, slots[...])
    text_unit, text_len = unit_rows(text_ref[...])
    text_grad_ref[...] = back_through_norm(text_unit, text_len, total)
    each(1, reply_copy, left)


def body(audio, text, labels, route, scale, bias):
    row_count, width = audio.shape
    wide_size = lax.axis_size("wide")
    side = math.isqrt(lax.axis_size("narrow"))
    slot_count = wide_size * CAPACITY
    vmem = pl.BlockSpec(memory_space=pltpu.VMEM)
    smem = pl.BlockSpec(memory_space=pltpu.SMEM)
    blocks = pltpu.VMEM((wide_size // 2, 2, CAPACITY * width // LANES, LANES), BF16)
    wide_labels = pltpu.VMEM((wide_size, 1, LANES), F32)
    gathered = pltpu.VMEM((side, row_count, width), BF16)
    gathered_labels = pltpu.VMEM((side, 1, row_count), F32)
    term = pltpu.VMEM((row_count, width), F32)
    parts = pltpu.VMEM((side - 1, row_count, width), BF16)
    part_losses = pltpu.VMEM((side - 1, 1, row_count), F32)
    far_sem = pltpu.SemaphoreType.DMA((wide_size,))
    near_sem = pltpu.SemaphoreType.DMA((7, side))
    row_loss, audio_grad, text_grad = pl.pallas_call(
        functools.partial(kernel, wide_size, side),
        out_shape=(
            jax.ShapeDtypeStruct((1, row_count), F32),
            jax.ShapeDtypeStruct((row_count, width), F32),
            jax.ShapeDtypeStruct((row_count, width), F32),
        ),
        in_specs=[smem, smem, vmem, vmem, vmem, vmem],
        out_specs=(vmem, vmem, vmem),
        scratch_shapes=[
            blocks, blocks, blocks, blocks, wide_labels, wide_labels,
            pltpu.VMEM((slot_count, width), BF16),
            gathered, gathered, gathered_labels, gathered_labels,
            pltpu.VMEM((side, side, row_count, row_count), BF16),
            term, term, pltpu.VMEM((1, row_count), F32),
            parts, parts, parts, parts, part_losses, part_losses,
            far_sem, far_sem, far_sem, far_sem, far_sem, far_sem,
            near_sem, near_sem, pltpu.SemaphoreType.DMA((2,)),
        ],
        compiler_params=pltpu.CompilerParams(
            collective_id=0, has_side_effects=True, vmem_limit_bytes=48 * 2**20
        ),
    )(scale, bias, audio, text, labels.reshape(1, row_count), route)
    return (row_loss.reshape(row_count), audio_grad, text_grad)


def solution(mesh):
    rows = P(("wide", "narrow"), None)
    return jax.shard_map(
        body,
        mesh=mesh,
        in_specs=(rows, rows, P(("wide", "narrow")), rows, P(), P()),
        out_specs=(P(("wide", "narrow")), rows, rows),
        check_vma=False,
    )
```

time: 320 us -> 155 us (0.48)
  waiting for transfers between devices: 221 us -> 0 us
  Pallas kernels: 0 us -> 148 us
  starting transfers between devices: 34.5 us -> 0 us
  blocking collectives: 17.2 us -> 0 us
  matrix products: 13.6 us -> 0 us
  between operations: 15.5 us -> 1.94 us
  other arithmetic: 11.1 us -> 0 us
    pallas_call x0 -> x1, Pallas kernels: none -> 148 us  [body(): pl.pallas_call(functools.partial(kernel, wide_size, side), out_shape=(jax...]
    all_to_all x3 -> x0, waiting for transfers between devices: 142 us -> none  [the longest x1 63 us: body(): lax.all_to_all(send_text, 'wide', split_axis=0, concat_axis=0, tiled=True)]
    all_gather x1 -> x0, waiting for transfers between devices: 78.7 us -> none  [body(): lax.all_gather(text_hat, 'narrow', axis=0, tiled=True)]
    all_to_all x3 -> x0, starting transfers between devices: 34.5 us -> none  [the longest x1 23.8 us: body(): lax.all_to_all(send_labels, 'wide', split_axis=0, concat_axis=0, tiled=True)]
    all_gather x1 -> x0, blocking collectives: 17.2 us -> none  [body(): lax.all_gather(labels, 'narrow', axis=0, tiled=True)]
    dot_general x6 -> x0, matrix products: 13.6 us -> none  [the longest x2 5.14 us: tile_terms(): jnp.dot(weights.T, audio_hat, preferred_element_type=jnp.float32)]
    unnamed x8 -> x12, local copies, waits for them, and re-layouts: 0.64 us -> 5.3 us
    reduce_sum x4 -> x0, other arithmetic: 3.61 us -> none  [the longest x2 2.17 us: unit_rows(): jnp.sum(values * values, axis=-1, keepdims=True) + EPSILON]
  transfers between devices with their start and end apart: 5 -> 0, of which waited for: 4 -> 0; matrix products, arithmetic and copies ran while one was open for 4% -> 0% of each run, Pallas kernels for 0% -> 0%
where the time goes in v1:
time: 155 us
  Pallas kernels  148 us (95%)
  local copies, waits for them, and re-layouts  5.3 us (3%)
  between operations  1.94 us (1%)
    pallas_call x1, Pallas kernels, body(): pl.pallas_call(functools.partial(kernel, wide_size, side), out_shape=(jax...  148 us
    unnamed x12, local copies, waits for them, and re-layouts  5.3 us

profile of v1, /device:TPU:1, one launch (start us, length us, event | category | flops | bytes accessed | tf_op | source)
XLA Modules:
  0.0 154.9 jit_solution(7065064338704066346)
XLA Ops:
  1.9 0.0 copy-start.3
  1.9 0.6 copy-done.3
  2.6 0.0 copy-start.2
  2.6 0.1 copy.9.route_ref
  2.7 0.5 copy-done.2
  3.2 0.0 copy-start
  3.2 0.9 copy-done
  4.2 0.0 copy-start.1
  4.2 0.9 copy-done.1
  5.1 147.7 %shard_map.85 = (f32[1,128]{1,0:T(1,128)S(1)}, f32[128,1024]{1,0:T(8,128)S(1)}, f32[128,1024]{1,0:T(8,128)S(1)}) custom-call(f32[1]{0:T(128)S(6)} %copy.13.scale_ref, f32[1]{0:T(128)S(6)} %copy.14.bias_ref, bf16[128,1024]{1,0:T(8,128)(2,1)S(1)} %copy-done, bf16[128,1024]{1,0:T(8,128)(2,1)S(1)} %copy-done.1, s32[1,128]{1,0:T(1,128)S(1)} %bitcast.2, ...), custom_call_target="tpu_custom_call" | custom-call | tf_op jit(solution)/shard_map/pallas_call | solution.py:349
  152.8 0.5 copy.15
  153.4 0.8 copy.16
  154.1 0.8 copy.17
Async XLA Ops:
  1.9 0.7 copy-start.3
  2.6 0.7 copy-start.2
  3.2 0.9 copy-start
  4.2 0.9 copy-start.1

commit v2 on v1

v2 whole, which is shorter than its diff:
```python
import functools
import math

import jax
import jax.numpy as jnp
from jax import lax
from jax.experimental import pallas as pl
from jax.experimental.pallas import tpu as pltpu
from jax.sharding import PartitionSpec as P

EPSILON = 1e-06
MESH = pl.DeviceIdType.MESH
LANES = 128
CAPACITY = 4
CHUNKS = 4
F32 = jnp.float32
BF16 = jnp.bfloat16


def unit_rows(raw):
    values = raw.astype(F32)
    length = jnp.sqrt(jnp.sum(values * values, axis=-1, keepdims=True) + EPSILON)
    return (values / length, length)


def back_through_norm(unit, length, grad):
    return (grad - unit * jnp.sum(unit * grad, axis=-1, keepdims=True)) / length


def dot_nt(a, b):
    return lax.dot_general(a, b, (((1,), (1,)), ((), ())), preferred_element_type=F32)


def dot_nn(a, b):
    return lax.dot_general(a, b, (((1,), (0,)), ((), ())), preferred_element_type=F32)


def dot_tn(a, b):
    return lax.dot_general(a, b, (((0,), (0,)), ((), ())), preferred_element_type=F32)


def iota(shape, axis):
    return lax.broadcasted_iota(jnp.int32, shape, axis)


def to_column(row):
    size = row.shape[1]
    eye = iota((size, size), 0) == iota((size, size), 1)
    return jnp.sum(jnp.where(eye, row, 0.0), axis=1, keepdims=True)


def to_row(column):
    size = column.shape[0]
    eye = iota((size, size), 0) == iota((size, size), 1)
    return jnp.sum(jnp.where(eye, column, 0.0), axis=0, keepdims=True)


def pair_terms(products, audio_labels, text_labels, scale, bias):
    logits = scale * products + bias
    matched = audio_labels == text_labels
    small = jnp.exp(-jnp.abs(logits))
    losses = jnp.maximum(jnp.where(matched, -logits, logits), 0.0) + jnp.log1p(small)
    sigmoid = jnp.where(logits >= 0.0, 1.0, small) / (1.0 + small)
    slope = sigmoid - jnp.where(matched, 1.0, 0.0)
    return (losses, slope)


def write_blocks(slab, out_ref, chunks, blocks):
    for half in range(chunks // 4):
        even, odd = [], []
        for g in (2 * half, 2 * half + 1):
            first, second = slab(2 * g), slab(2 * g + 1)
            first = first.reshape(-1, 8, LANES)
            second = second.reshape(-1, 8, LANES)
            low = iota(first.shape, 1) < CAPACITY
            even.append(jnp.where(low, first, pltpu.roll(second, CAPACITY, 1)))
            odd.append(jnp.where(low, pltpu.roll(first, CAPACITY, 1), second))
        rows = pl.ds(16 * half, 16)
        out_ref[blocks, 0, rows, :] = jnp.concatenate(even, axis=1).astype(BF16)
        out_ref[blocks, 1, rows, :] = jnp.concatenate(odd, axis=1).astype(BF16)


def read_blocks(in_ref, out_ref, chunks, blocks):
    span = pl.ds(blocks.start * 2 * CAPACITY, blocks.size * 2 * CAPACITY)
    for half in range(chunks // 4):
        rows = pl.ds(16 * half, 16)
        even = in_ref[blocks, 0, rows, :].astype(F32)
        odd = in_ref[blocks, 1, rows, :].astype(F32)
        for step in range(2):
            g = 2 * half + step
            e = even[:, 8 * step : 8 * step + 8, :]
            o = odd[:, 8 * step : 8 * step + 8, :]
            low = iota(e.shape, 1) < CAPACITY
            first = jnp.where(low, e, pltpu.roll(o, CAPACITY, 1))
            second = jnp.where(low, pltpu.roll(e, CAPACITY, 1), o)
            out_ref[span, pl.ds(2 * g * LANES, LANES)] = first.reshape(-1, LANES).astype(BF16)
            out_ref[span, pl.ds((2 * g + 1) * LANES, LANES)] = second.reshape(-1, LANES).astype(BF16)


def kernel(
    wide_size, side,
    scale_ref, bias_ref, audio_hbm, text_hbm, labels_hbm, route_hbm,
    loss_ref, audio_grad_ref, text_grad_ref,
    audio_ref, text_ref, labels_ref, route_ref,
    out_rows, in_rows, out_reply, in_reply, spare, slots,
    out_near, in_near, out_far, in_far,
    audio_all, text_all, audio_labels, text_labels,
    weights, audio_sum, text_sum, loss_sum,
    audio_out, audio_in, text_out, text_in, loss_out, loss_in,
    rows_send, rows_recv, reply_send, reply_recv,
    labels_send, labels_recv, near_send, near_recv, local_sem,
):
    row_count, width = audio_ref.shape
    chunks = width // LANES
    group = row_count * side * side
    slot_count = wide_size * CAPACITY
    pairs = wide_size // 2 // CHUNKS
    w = lax.axis_index("wide")
    n = lax.axis_index("narrow")
    y, x = n // side, n % side
    scale, bias = scale_ref[0], bias_ref[0]

    loads = [
        pltpu.make_async_copy(src, dst, local_sem.at[i])
        for i, (src, dst) in enumerate(
            [(text_hbm, text_ref), (route_hbm, route_ref), (labels_hbm, labels_ref), (audio_hbm, audio_ref)]
        )
    ]
    for load in loads:
        load.start()

    def ahead(k):
        return lax.rem(w + k, wide_size)

    def along_x(d):
        return lax.rem(x + d, side)

    def along_y(d):
        return lax.rem(y + d, side)

    def offset(p):
        q = wide_size - 1 - p
        return jnp.where(lax.rem(q, 2) == 0, q // 2, wide_size - 1 - q // 2)

    barrier = pltpu.get_barrier_semaphore()

    def greet(k, carry):
        pl.semaphore_signal(barrier, inc=1, device_id=(ahead(k), n), device_id_type=MESH)
        return carry

    lax.fori_loop(1, wide_size, greet, 0)
    for d in range(1, side):
        pl.semaphore_signal(barrier, inc=1, device_id=(w, y * side + along_x(d)), device_id_type=MESH)
        pl.semaphore_signal(barrier, inc=1, device_id=(w, along_y(d) * side + x), device_id_type=MESH)

    loads[0].wait()
    text_hat = unit_rows(text_ref[...])[0].astype(BF16)
    text_all[y] = text_hat
    loads[1].wait()
    target_row = route_ref[...]
    target = to_column(target_row.astype(F32)).astype(jnp.int32)
    square = (row_count, row_count)
    same = target == target_row
    before = iota(square, 0) < iota(square, 1)
    after = iota(square, 0) > iota(square, 1)
    rank_row = jnp.sum(jnp.where(same & before, 1.0, 0.0), axis=0, keepdims=True).astype(jnp.int32)
    rank = jnp.sum(jnp.where(same & after, 1.0, 0.0), axis=1, keepdims=True).astype(jnp.int32)

    def place_of(holder, source):
        k = holder - source
        k = jnp.where(k < 0, k + wide_size, k)
        return wide_size - 1 - jnp.where(k < wide_size // 2, 2 * k, 2 * (wide_size - k) - 1)

    slot_row = place_of(target_row, w) * CAPACITY + rank_row
    slot_column = place_of(target, w) * CAPACITY + rank
    pick = jnp.where(iota((slot_count, row_count), 0) == slot_row, 1.0, 0.0).astype(BF16)
    every = pl.ds(0, wide_size // 2)
    write_blocks(lambda c: dot_nn(pick, text_hat[:, c * LANES : (c + 1) * LANES]), out_rows, chunks, every)

    inner = 8 if wide_size >= 64 else 2
    outer = wide_size // inner
    a, b = w // inner, w % inner
    loads[2].wait()
    label_row = labels_ref[...].astype(F32)
    text_labels[y] = label_row
    audio_labels[x] = label_row
    label_column = to_column(label_row)
    label_lane = (target // inner) * CAPACITY + rank
    spread = jnp.where(iota((row_count, LANES), 1) == label_lane, label_column + 1.0, 0.0)
    for e in range(inner):
        found = jnp.where(target % inner == e, spread, 0.0)
        out_near[e] = jnp.sum(found, axis=0, keepdims=True) - 1.0
    in_near[b] = out_near[b]

    pl.semaphore_wait(barrier, wide_size - 1 + 2 * (side - 1))

    def wide_copy(src, dst, send, recv, peer):
        return pltpu.make_async_remote_copy(
            src_ref=src, dst_ref=dst, send_sem=send, recv_sem=recv, device_id=(peer, n), device_id_type=MESH
        )

    label_steps = []
    for e in range(1, inner):
        f = lax.rem(b + e, inner)
        label_steps.append(
            wide_copy(out_near.at[f], in_near.at[b], labels_send.at[0, e], labels_recv.at[0, e], a * inner + f)
        )
    for copy in label_steps:
        copy.start()

    def start_blocks(src, dst, send, recv, chunk, sign):
        def step(p, carry):
            peer = lax.rem(w + wide_size + sign * offset(p), wide_size)
            wide_copy(src.at[p // 2, p % 2], dst.at[p // 2, p % 2], send.at[0], recv.at[chunk], peer).start()
            return carry

        first = chunk * 2 * pairs
        lax.fori_loop(first, min(first + 2 * pairs, wide_size - 1), step, 0)
        if chunk == CHUNKS - 1:
            pltpu.make_async_copy(src.at[wide_size // 2 - 1, 1], dst.at[wide_size // 2 - 1, 1], recv.at[CHUNKS - 1]).start()
            pltpu.make_async_copy(src.at[wide_size // 2 - 1, 1], spare.at[(1 - sign) // 2], send.at[0]).start()

    def wait_blocks(dst, recv, chunk):
        whole = dst.at[pl.ds(chunk * pairs, pairs)]
        pltpu.make_async_copy(whole, whole, recv.at[chunk]).wait()

    start_blocks(out_rows, in_rows, rows_send, rows_recv, 0, 1)

    def near_copy(kind, src, dst, d, on_x):
        peer = y * side + along_x(d) if on_x else along_y(d) * side + x
        return pltpu.make_async_remote_copy(
            src_ref=src,
            dst_ref=dst,
            send_sem=near_send.at[kind, d],
            recv_sem=near_recv.at[kind, d],
            device_id=(w, peer),
            device_id_type=MESH,
        )

    near = []
    for d in range(1, side):
        near.append(near_copy(0, text_all.at[y], text_all.at[y], d, False))
        near.append(near_copy(1, text_labels.at[y], text_labels.at[y], d, False))
        near.append(near_copy(2, audio_labels.at[x], audio_labels.at[x], d, True))
    for copy in near:
        copy.start()
    loads[3].wait()
    audio_hat = unit_rows(audio_ref[...])[0].astype(BF16)
    audio_all[x] = audio_hat
    shared = [near_copy(3, audio_all.at[x], audio_all.at[x], d, True) for d in range(1, side)]
    for copy in shared:
        copy.start()
    near += shared

    for copy in label_steps:
        copy.wait_recv()
    heard = in_near[...].reshape(inner, LANES)
    turned = {d: pltpu.roll(heard, (d * CAPACITY) % LANES, 1) for d in range(1 - outer, inner)}
    source = iota((inner, LANES), 0)
    mine = iota((inner, LANES), 1) // CAPACITY == source
    for h in range(outer):
        row = jnp.zeros((inner, LANES), F32)
        for e in range(inner):
            row = jnp.where(mine & (source == e), turned[e - h], row)
        out_far[h] = jnp.sum(row, axis=0, keepdims=True)
    in_far[a] = out_far[a]
    for d in range(1, outer):
        h = lax.rem(a + d, outer)
        label_steps.append(
            wide_copy(out_far.at[h], in_far.at[a], labels_send.at[1, d], labels_recv.at[1, d], h * inner + b)
        )
        label_steps[-1].start()
    for chunk in range(1, CHUNKS):
        start_blocks(out_rows, in_rows, rows_send, rows_recv, chunk, 1)

    for copy in near:
        copy.wait_recv()

    block_rows = side * row_count
    text_block = text_all[...].reshape(block_rows, width)
    column_labels = jnp.concatenate([text_labels[t] for t in range(side)], axis=1)
    sent = []
    for d in range(side):
        owner = along_x(d)
        rows = audio_all[owner]
        losses, slope = pair_terms(
            dot_nt(rows, text_block), to_column(audio_labels[owner]), column_labels, scale, bias
        )
        block = (scale * slope).astype(BF16)
        for t in range(side):
            weights[t, owner] = block[:, t * row_count : (t + 1) * row_count]
        grad = dot_nn(block, text_block)
        loss = to_row(jnp.sum(losses, axis=1, keepdims=True))
        if d == 0:
            audio_sum[...] = grad
            loss_sum[...] = loss
        else:
            audio_out[d - 1] = grad.astype(BF16)
            loss_out[d - 1] = loss
            sent.append(near_copy(4, audio_out.at[d - 1], audio_in.at[d - 1], d, True))
            sent.append(near_copy(5, loss_out.at[d - 1], loss_in.at[d - 1], d, True))
            sent[-2].start()
            sent[-1].start()
    audio_block = audio_all[...].reshape(block_rows, width)
    for d in range(side):
        grad = dot_tn(weights[along_y(d)].reshape(block_rows, row_count), audio_block)
        if d == 0:
            text_sum[...] = grad
        else:
            text_out[d - 1] = grad.astype(BF16)
            sent.append(near_copy(6, text_out.at[d - 1], text_in.at[d - 1], d, False))
            sent[-1].start()

    for copy in label_steps[inner - 1 :]:
        copy.wait_recv()
    share = inner * CAPACITY
    per_row = max(1, LANES // share)
    pieces = []
    for first in range(0, outer, per_row):
        row = jnp.zeros((1, LANES), F32)
        for h in range(first, min(first + per_row, outer)):
            moved = pltpu.roll(in_far[h], ((h - first) * share) % LANES, 1)
            row = jnp.where(iota((1, LANES), 1) // share == h - first, moved, row)
        pieces.append(row)
    by_source = jnp.concatenate(pieces, axis=1)[:, :slot_count]
    slot = iota((slot_count, slot_count), 0)
    here = place_of(w, slot // CAPACITY) * CAPACITY + slot % CAPACITY
    moved = jnp.where(here == iota((slot_count, slot_count), 1), to_column(by_source), 0.0)
    slot_labels = jnp.sum(moved, axis=0, keepdims=True)
    own_audio = audio_all[x]
    own_labels = to_column(audio_labels[x])
    for chunk in range(CHUNKS):
        span = slice(chunk * 2 * pairs * CAPACITY, (chunk + 1) * 2 * pairs * CAPACITY)
        blocks = pl.ds(chunk * pairs, pairs)
        labels = slot_labels[:, span]
        present = labels >= 0.0
        wait_blocks(in_rows, rows_recv, chunk)
        read_blocks(in_rows, slots, chunks, blocks)
        held = slots[span]
        losses, slope = pair_terms(dot_nt(own_audio, held), own_labels, labels, scale, bias)
        routed = (scale * jnp.where(present, slope, 0.0)).astype(BF16)
        write_blocks(
            lambda c: dot_tn(routed, audio_all[x, :, pl.ds(c * LANES, LANES)]), out_reply, chunks, blocks
        )
        start_blocks(out_reply, in_reply, reply_send, reply_recv, chunk, -1)
        loss_sum[...] += to_row(jnp.sum(jnp.where(present, losses, 0.0), axis=1, keepdims=True))
        audio_sum[...] += dot_nn(routed, held)

    for copy in sent:
        copy.wait_recv()
    total = audio_sum[...]
    loss = loss_sum[...]
    for d in range(side - 1):
        total += audio_in[d].astype(F32)
        loss += loss_in[d]
    loss_ref[...] = loss / group
    audio_unit, audio_len = unit_rows(audio_ref[...])
    audio_grad_ref[...] = back_through_norm(audio_unit, audio_len, total)
    for d in range(side - 1):
        text_sum[...] += text_in[d].astype(F32)
    for copy in near + sent + label_steps:
        copy.wait_send()
    pltpu.make_async_copy(out_rows, out_rows, rows_send.at[0]).wait()

    pick_back = jnp.where(iota((row_count, slot_count), 1) == slot_column, 1.0, 0.0).astype(BF16)
    total = text_sum[...]
    for chunk in range(CHUNKS):
        span = slice(chunk * 2 * pairs * CAPACITY, (chunk + 1) * 2 * pairs * CAPACITY)
        wait_blocks(in_reply, reply_recv, chunk)
        read_blocks(in_reply, slots, chunks, pl.ds(chunk * pairs, pairs))
        total += dot_nn(pick_back[:, span], slots[span])
    text_unit, text_len = unit_rows(text_ref[...])
    text_grad_ref[...] = back_through_norm(text_unit, text_len, total)
    pltpu.make_async_copy(out_reply, out_reply, reply_send.at[0]).wait()


def body(audio, text, labels, route, scale, bias):
    row_count, width = audio.shape
    wide_size = lax.axis_size("wide")
    side = math.isqrt(lax.axis_size("narrow"))
    slot_count = wide_size * CAPACITY
    vmem = pl.BlockSpec(memory_space=pltpu.VMEM)
    smem = pl.BlockSpec(memory_space=pltpu.SMEM)
    blocks = pltpu.VMEM((wide_size // 2, 2, CAPACITY * width // LANES, LANES), BF16)
    inner = 8 if wide_size >= 64 else 2
    near_labels = pltpu.VMEM((inner, 1, LANES), F32)
    far_labels = pltpu.VMEM((wide_size // inner, 1, LANES), F32)
    rows = pltpu.VMEM((row_count, width), BF16)
    numbers = pltpu.VMEM((1, row_count), jnp.int32)
    whole = pl.BlockSpec(memory_space=pl.ANY)
    gathered = pltpu.VMEM((side, row_count, width), BF16)
    gathered_labels = pltpu.VMEM((side, 1, row_count), F32)
    term = pltpu.VMEM((row_count, width), F32)
    parts = pltpu.VMEM((side - 1, row_count, width), BF16)
    part_losses = pltpu.VMEM((side - 1, 1, row_count), F32)
    one_sem = pltpu.SemaphoreType.DMA((1,))
    chunk_sem = pltpu.SemaphoreType.DMA((CHUNKS,))
    label_sem = pltpu.SemaphoreType.DMA((2, max(inner, wide_size // inner)))
    near_sem = pltpu.SemaphoreType.DMA((7, side))
    row_loss, audio_grad, text_grad = pl.pallas_call(
        functools.partial(kernel, wide_size, side),
        out_shape=(
            jax.ShapeDtypeStruct((1, row_count), F32),
            jax.ShapeDtypeStruct((row_count, width), F32),
            jax.ShapeDtypeStruct((row_count, width), F32),
        ),
        in_specs=[smem, smem, whole, whole, whole, whole],
        out_specs=(vmem, vmem, vmem),
        scratch_shapes=[
            rows, rows, numbers, numbers,
            blocks, blocks, blocks, blocks, pltpu.VMEM((2, CAPACITY * width // LANES, LANES), BF16),
            pltpu.VMEM((slot_count, width), BF16),
            near_labels, near_labels, far_labels, far_labels,
            gathered, gathered, gathered_labels, gathered_labels,
            pltpu.VMEM((side, side, row_count, row_count), BF16),
            term, term, pltpu.VMEM((1, row_count), F32),
            parts, parts, parts, parts, part_losses, part_losses,
            one_sem, chunk_sem, one_sem, chunk_sem,
            label_sem, label_sem, near_sem, near_sem, pltpu.SemaphoreType.DMA((4,)),
        ],
        compiler_params=pltpu.CompilerParams(
            collective_id=0, has_side_effects=True, vmem_limit_bytes=56 * 2**20
        ),
    )(scale, bias, audio, text, labels.reshape(1, row_count), route.reshape(1, row_count))
    return (row_loss.reshape(row_count), audio_grad, text_grad)


def solution(mesh):
    rows = P(("wide", "narrow"), None)
    return jax.shard_map(
        body,
        mesh=mesh,
        in_specs=(rows, rows, P(("wide", "narrow")), rows, P(), P()),
        out_specs=(P(("wide", "narrow")), rows, rows),
        check_vma=False,
    )
```

time: 155 us -> 130 us (0.84)
  Pallas kernels: 148 us -> 124 us
    pallas_call x1, Pallas kernels: 148 us -> 124 us  [body(): pl.pallas_call(functools.partial(kernel, wide_size, side), out_shape=(jax...]
    unnamed x12 -> x7, local copies, waits for them, and re-layouts: 5.3 us -> 3.91 us
where the time goes in v2:
time: 130 us
  Pallas kernels  124 us (95%)
  local copies, waits for them, and re-layouts  3.91 us (3%)
  between operations  1.94 us (1%)
    pallas_call x1, Pallas kernels, body(): pl.pallas_call(functools.partial(kernel, wide_size, side), out_shape=(jax...  124 us
    unnamed x7, local copies, waits for them, and re-layouts  3.91 us

profile of v2, /device:TPU:1, one launch (start us, length us, event | category | flops | bytes accessed | tf_op | source)
XLA Modules:
  0.0 130.1 jit_solution(577862483708553051)
XLA Ops:
  1.9 124.2 %shard_map.85 = (f32[1,128]{1,0:T(1,128)}, f32[128,1024]{1,0:T(8,128)}, f32[128,1024]{1,0:T(8,128)}) custom-call(f32[1]{0:T(128)S(6)} %copy.12.scale_ref, f32[1]{0:T(128)S(6)} %copy.13.bias_ref, bf16[128,1024]{1,0:T(8,128)(2,1)} %audio_hbm.1, bf16[128,1024]{1,0:T(8,128)(2,1)} %text_hbm.1, s32[1,128]{1,0:T(1,128)} %bitcast.3, s32[1,128]{1,0:T(1,128)} %bitcast.4), custom_call_target="tpu_custom_call" | custom-call | tf_op jit(solution)/shard_map/pallas_call | solution.py:400
  126.2 0.0 copy-start.1
  126.2 0.7 copy-done.1
  126.8 0.5 copy.14
  127.3 0.0 copy-start
  127.3 1.9 %copy.15 = f32[128,1024]{1,0:T(8,128)} copy(f32[128,1024]{1,0:T(8,128)} %get-tuple-element.13) | data formatting | bytes 1048576
  129.3 0.0 copy-done
  129.3 0.8 copy.16
Async XLA Ops:
  126.2 0.7 copy-start.1
  127.3 1.9 %copy-start = (f32[128,1024]{1,0:T(8,128)S(1)}, f32[128,1024]{1,0:T(8,128)}, u32[]{:S(2)}) copy-start(f32[128,1024]{1,0:T(8,128)} %get-tuple-element.14) | copy-start | bytes 1572868

commit v3 on v2

--- a/solution.py
+++ b/solution.py
@@ -13,6 +13,7 @@
 LANES = 128
 CAPACITY = 4
 CHUNKS = 4
+EARLY = 8
 F32 = jnp.float32
 BF16 = jnp.bfloat16
 
@@ -171,8 +172,22 @@
         k = jnp.where(k < 0, k + wide_size, k)
         return wide_size - 1 - jnp.where(k < wide_size // 2, 2 * k, 2 * (wide_size - k) - 1)
 
-    slot_row = place_of(target_row, w) * CAPACITY + rank_row
-    slot_column = place_of(target, w) * CAPACITY + rank
+    half, quarter = wide_size // 2, wide_size // 4
+
+    def swapped(p, device, other, late):
+        i = p - quarter
+        back = late(i)
+        p = jnp.where((i >= 0) & (i < EARLY) & (device >= EARLY) & (back >= half), back, p)
+        return jnp.where((i >= quarter) & (other < EARLY) & (device >= EARLY), quarter + other, p)
+
+    def sender_place(p, source, holder):
+        return swapped(p, source, holder, lambda i: place_of(i, source))
+
+    def holder_place(p, holder, source):
+        return swapped(p, holder, source, lambda i: place_of(holder, i))
+
+    slot_row = sender_place(place_of(target_row, w), w, target_row) * CAPACITY + rank_row
+    slot_column = sender_place(place_of(target, w), w, target) * CAPACITY + rank
     pick = jnp.where(iota((slot_count, row_count), 0) == slot_row, 1.0, 0.0).astype(BF16)
     every = pl.ds(0, wide_size // 2)
     write_blocks(lambda c: dot_nn(pick, text_hat[:, c * LANES : (c + 1) * LANES]), out_rows, chunks, every)
@@ -210,15 +225,26 @@
 
     def start_blocks(src, dst, send, recv, chunk, sign):
         def step(p, carry):
-            peer = lax.rem(w + wide_size + sign * offset(p), wide_size)
-            wide_copy(src.at[p // 2, p % 2], dst.at[p // 2, p % 2], send.at[0], recv.at[chunk], peer).start()
+            if sign > 0:
+                place = sender_place(p, w, ahead(offset(p)))
+                peer = ahead(offset(place))
+                there = holder_place(place, peer, w)
+            else:
+                place = holder_place(p, w, ahead(wide_size - offset(p)))
+                peer = ahead(wide_size - offset(place))
+                there = sender_place(place, peer, w)
+            wide_copy(
+                src.at[p // 2, p % 2], dst.at[there // 2, there % 2], send.at[0], recv.at[there // (2 * pairs)], peer
+            ).start()
             return carry
 
+        own = wide_size - 1
         first = chunk * 2 * pairs
-        lax.fori_loop(first, min(first + 2 * pairs, wide_size - 1), step, 0)
+        lax.fori_loop(first, min(first + 2 * pairs, own), step, 0)
         if chunk == CHUNKS - 1:
-            pltpu.make_async_copy(src.at[wide_size // 2 - 1, 1], dst.at[wide_size // 2 - 1, 1], recv.at[CHUNKS - 1]).start()
-            pltpu.make_async_copy(src.at[wide_size // 2 - 1, 1], spare.at[(1 - sign) // 2], send.at[0]).start()
+            block = src.at[own // 2, own % 2]
+            pltpu.make_async_copy(block, dst.at[own // 2, own % 2], recv.at[chunk]).start()
+            pltpu.make_async_copy(block, spare.at[(1 - sign) // 2], send.at[0]).start()
 
     def wait_blocks(dst, recv, chunk):
         whole = dst.at[pl.ds(chunk * pairs, pairs)]
@@ -324,7 +350,7 @@
         pieces.append(row)
     by_source = jnp.concatenate(pieces, axis=1)[:, :slot_count]
     slot = iota((slot_count, slot_count), 0)
-    here = place_of(w, slot // CAPACITY) * CAPACITY + slot % CAPACITY
+    here = holder_place(place_of(w, slot // CAPACITY), w, slot // CAPACITY) * CAPACITY + slot % CAPACITY
     moved = jnp.where(here == iota((slot_count, slot_count), 1), to_column(by_source), 0.0)
     slot_labels = jnp.sum(moved, axis=0, keepdims=True)
     own_audio = audio_all[x]

time: 130 us -> 126 us (0.969)
  Pallas kernels: 124 us -> 120 us
    pallas_call x1, Pallas kernels: 124 us -> 120 us  [body(): pl.pallas_call(functools.partial(kernel, wide_size, side), out_shape=(jax...]
where the time goes in v3:
time: 126 us
  Pallas kernels  120 us (95%)
  local copies, waits for them, and re-layouts  3.91 us (3%)
  between operations  1.94 us (2%)
    pallas_call x1, Pallas kernels, body(): pl.pallas_call(functools.partial(kernel, wide_size, side), out_shape=(jax...  120 us
    unnamed x7, local copies, waits for them, and re-layouts  3.91 us

profile of v3, /device:TPU:1, one launch (start us, length us, event | category | flops | bytes accessed | tf_op | source)
XLA Modules:
  0.0 126.2 jit_solution(2520388554544625509)
XLA Ops:
  1.9 120.4 %shard_map.85 = (f32[1,128]{1,0:T(1,128)}, f32[128,1024]{1,0:T(8,128)}, f32[128,1024]{1,0:T(8,128)}) custom-call(f32[1]{0:T(128)S(6)} %copy.12.scale_ref, f32[1]{0:T(128)S(6)} %copy.13.bias_ref, bf16[128,1024]{1,0:T(8,128)(2,1)} %audio_hbm.1, bf16[128,1024]{1,0:T(8,128)(2,1)} %text_hbm.1, s32[1,128]{1,0:T(1,128)} %bitcast.3, s32[1,128]{1,0:T(1,128)} %bitcast.4), custom_call_target="tpu_custom_call" | custom-call | tf_op jit(solution)/shard_map/pallas_call | solution.py:426
  122.3 0.0 copy-start.1
  122.3 0.7 copy-done.1
  123.0 0.5 copy.14
  123.5 0.0 copy-start
  123.5 1.9 %copy.15 = f32[128,1024]{1,0:T(8,128)} copy(f32[128,1024]{1,0:T(8,128)} %get-tuple-element.13) | data formatting | bytes 1048576
  125.4 0.0 copy-done
  125.4 0.8 copy.16
Async XLA Ops:
  122.3 0.7 copy-start.1
  123.5 1.9 %copy-start = (f32[128,1024]{1,0:T(8,128)S(1)}, f32[128,1024]{1,0:T(8,128)}, u32[]{:S(2)}) copy-start(f32[128,1024]{1,0:T(8,128)} %get-tuple-element.14) | copy-start | bytes 1572868
